TPU v7x, 512 devices: a whole 4x8x8 slice. The times are simulated.
512 devices in a mesh: ep: 128 (over z, y, core), dp: 4 (over x).
Axes of the slice: x: 4, y: 8, z: 8, core: 2. Of those that a mesh axis runs over, the one named last changes fastest.
Arguments:
- tokens: bfloat16 [65536, 2048], P(('dp', 'ep')), parts along dimension 0, may hold values from -6 to 6
- expert_ids: int32 [65536, 4], P(('dp', 'ep')), parts along dimension 0, may hold values from 0 to 127, all different within a row; in each aligned block of 128 rows (0 to 127, 128 to 255, ...) at most 6 rows name the same one
- gate_values: float32 [65536, 4], P(('dp', 'ep')), parts along dimension 0, may hold values from 0.1 to 1
- latent_down: bfloat16 [2048, 512], P('ep'), may hold values from -0.125 to 0.125
- latent_up: bfloat16 [512, 2048], P(None, 'ep'), may hold values from -0.25 to 0.25
- expert_up: bfloat16 [128, 512, 1408], P('ep'), may hold values from -0.25 to 0.25
- expert_down: bfloat16 [128, 1408, 512], P('ep'), may hold values from -0.15625 to 0.15625
- grad_out: bfloat16 [65536, 2048], P(('dp', 'ep')), parts along dimension 0, may hold values from -6 to 6
Outputs:
- layer_out: bfloat16 [65536, 2048], P(('dp', 'ep')), parts along dimension 0
- grad_tokens: bfloat16 [65536, 2048], P(('dp', 'ep')), parts along dimension 0
There are 4 independent parts, one for each index of `dp`. A program takes and returns all parts, laid end to end along the dimension named above; an argument that names none is the same for every part. Nothing has to cross between parts.
Inputs may be any that keep to these rules, and one draw needn't show every extreme that they name: `expert_ids`: each row names 4 different experts. Among the 128 tokens of one device, no expert is named by more than 6 tokens, and in every draw some expert is named by exactly 6 tokens of some device.
All inputs are finite; a program needn't handle non-finite values.
Results may differ from a plain program's by a relative error of at most 0.013.
Values may be sent and summed in bfloat16 or wider, within the bound.
No kernel may reach another device: no remote copies, remote signals or barrier semaphores. Data moves between devices by JAX's collectives and lax.ppermute only.
A program may use at most 64 MiB of HBM per device.

v0:
```python
import jax
import jax.numpy as jnp
from jax import lax
from jax.sharding import PartitionSpec as P


def contract_last(left, right):
    return lax.dot_general(
        left, right, (((1,), (1,)), ((), ())), preferred_element_type=jnp.float32
    )


def on_device(
    tokens, expert_ids, gate_values, latent_down, latent_up, expert_up, expert_down, grad_out
):
    ep_size = lax.axis_size("ep")
    tok_rows = expert_ids.shape[0]
    top_count = expert_ids.shape[1]
    local_experts = expert_up.shape[0]
    width = latent_up.shape[0]
    experts = local_experts * ep_size
    capacity = max(2, (3 * tok_rows * top_count + 2 * experts - 1) // (2 * experts))
    full_down, full_up = (
        lax.all_gather(latent_down, "ep", axis=0, tiled=True),
        lax.all_gather(latent_up, "ep", axis=1, tiled=True),
    )
    latent = jnp.dot(tokens, full_down, preferred_element_type=jnp.float32).astype(jnp.bfloat16)
    numbers = jnp.arange(experts, dtype=jnp.int32)
    picked = (expert_ids[:, :, None] == numbers[None, None, :]).astype(jnp.int32)
    routed = jnp.sum(picked, axis=1)
    before = jnp.cumsum(routed, axis=0) - routed
    slot_pos = jnp.sum(picked * before[:, None, :], axis=2)
    flat_slot = expert_ids * capacity + slot_pos
    positions = jnp.arange(experts * capacity, dtype=jnp.int32)
    matches = flat_slot[None, :, :] == positions[:, None, None]
    placing = jnp.any(matches, axis=2).astype(jnp.bfloat16)
    gate_place = jnp.sum(jnp.where(matches, gate_values[None, :, :], 0.0), axis=2)
    outbound = jnp.dot(placing, latent, preferred_element_type=jnp.float32).astype(jnp.bfloat16)
    outbound = outbound.reshape(ep_size, local_experts, capacity, width)
    pre_act = jnp.einsum(
        "sjml,jlf->sjmf",
        lax.all_to_all(outbound, "ep", split_axis=0, concat_axis=0, tiled=True),
        expert_up,
        preferred_element_type=jnp.float32,
    )
    squared = jnp.square(jax.nn.relu(pre_act)).astype(jnp.bfloat16)
    expert_out = jnp.einsum(
        "sjmf,jfl->sjml", squared, expert_down, preferred_element_type=jnp.float32
    ).astype(jnp.bfloat16)
    expert_out, stored = (expert_out, pre_act)
    returned = lax.all_to_all(expert_out, "ep", split_axis=0, concat_axis=0, tiled=True).reshape(
        experts * capacity, width
    )
    gathered_rows = jnp.take(returned, flat_slot, axis=0)
    combined = jnp.sum(gate_values[:, :, None] * gathered_rows.astype(jnp.float32), axis=1).astype(
        jnp.bfloat16
    )
    layer_full = jnp.dot(combined, full_up, preferred_element_type=jnp.float32)
    grad_latent = contract_last(grad_out, full_up)
    layer_out = layer_full.astype(jnp.bfloat16)
    grad_send = jnp.dot(
        gate_place, grad_latent, precision=lax.Precision.HIGHEST, preferred_element_type=jnp.float32
    )
    grad_send = grad_send.astype(jnp.bfloat16).reshape(ep_size, local_experts, capacity, width)
    grad_arrived = lax.all_to_all(grad_send, "ep", split_axis=0, concat_axis=0, tiled=True)
    pre_act = stored
    grad_act = jnp.einsum(
        "sjml,jfl->sjmf", grad_arrived, expert_down, preferred_element_type=jnp.float32
    )
    grad_pre = (2.0 * jax.nn.relu(pre_act) * grad_act).astype(jnp.bfloat16)
    grad_in = jnp.einsum(
        "sjmf,jlf->sjml", grad_pre, expert_up, preferred_element_type=jnp.float32
    ).astype(jnp.bfloat16)
    grad_back = lax.all_to_all(grad_in, "ep", split_axis=0, concat_axis=0, tiled=True).reshape(
        experts * capacity, width
    )
    grad_sum = jnp.sum(jnp.take(grad_back, flat_slot, axis=0).astype(jnp.float32), axis=1).astype(
        jnp.bfloat16
    )
    grad_tokens = contract_last(grad_sum, full_down).astype(jnp.bfloat16)
    return (layer_out, grad_tokens)


def solution(mesh):
    placed = (
        P(("dp", "ep"), None),
        P(("dp", "ep"), None),
        P(("dp", "ep"), None),
        P("ep", None),
        P(None, "ep"),
        P("ep", None, None),
        P("ep", None, None),
        P(("dp", "ep"), None),
    )
    return jax.shard_map(
        on_device,
        mesh=mesh,
        in_specs=placed,
        out_specs=(P(("dp", "ep"), None), P(("dp", "ep"), None)),
        check_vma=False,
    )
```

profile of v0, /device:TPU:1, one launch (start us, length us, event | category | flops | bytes accessed | tf_op | source)
XLA Modules:
  0.0 342.6 jit_solution(10094555136022475105)
XLA Ops:
  7.2 0.0 copy-start
  7.2 0.0 all-gather.3.cloned.1.call-start
  7.2 0.7 all-gather.3.cloned.1.call-update
  7.9 0.0 all-gather.5.cloned.1.call-start
  8.0 0.7 all-gather.5.cloned.1.call-update
  8.7 0.8 convert_reduce_fusion
  9.5 0.2 reduce_window_sum.11
  9.7 0.9 select_reduce_fusion.2
  10.6 1.2 compare_and_fusion
  11.8 0.2 fusion.2
  12.0 87.9 %all-gather.3.cloned.1.call-done = bf16[2048,512]{1,0:T(8,128)(2,1)} async-done(((bf16[16,512]{1,0:T(8,128)(2,1)}), bf16[2048,512]{1,0:T(8,128)(2,1)}) %all-gather.3.cloned.1.call-update) | async-done | bytes 2097168 | tf_op jit(solution)/shard_map/all_gather | solution.py:24
  99.9 2.6 convolution_convert_fusion.3
  102.5 0.0 copy-start.5
  102.5 0.0 copy-start.4
  102.5 1.2 reshape.66
  103.8 9.5 %all-to-all-start = ((bf16[128,1,6,512]{3,2,1,0:T(8,128)(2,1)}), bf16[128,1,6,512]{3,2,1,0:T(8,128)(2,1)S(1)}, u32[]{:S(2)}, u32[]{:S(2)}) async-start(bf16[128,1,6,512]{3,2,1,0:T(8,128)(2,1)} %bitcast), calls=%async_computation | async-start | bytes 2097152 | tf_op jit(solution)/shard_map/all_to_all | solution.py:42
  113.3 0.0 copy-done.5
  113.3 0.9 select_reduce_fusion
  114.2 81.3 %all-gather.5.cloned.1.call-done = bf16[512,2048]{0,1:T(8,128)(2,1)} async-done(((bf16[512,16]{0,1:T(8,128)(2,1)}), bf16[512,2048]{0,1:T(8,128)(2,1)}) %all-gather.5.cloned.1.call-update) | async-done | bytes 2097168 | tf_op jit(solution)/shard_map/all_gather | solution.py:25
  195.5 0.0 copy-done.4
  195.5 0.0 copy-start.3
  195.5 2.1 fusion.33
  197.6 0.0 copy-done.3
  197.6 1.4 convolution_convert_fusion.2
  199.0 1.3 reshape.71
  200.3 0.0 all-to-all-done
  200.3 9.5 %all-to-all-start.2 = ((bf16[128,1,6,512]{3,2,1,0:T(8,128)(2,1)}), bf16[128,1,6,512]{3,2,1,0:T(8,128)(2,1)S(1)}, u32[]{:S(2)}, u32[]{:S(2)}) async-start(bf16[128,1,6,512]{3,2,1,0:T(8,128)(2,1)} %bitcast.9), calls=%async_computation.2 | async-start | bytes 2097152 | tf_op jit(solution)/shard_map/all_to_all | solution.py:65
  209.9 0.0 copy-done
  209.9 3.4 fusion.7
  213.3 27.5 %all-to-all-done.2 = bf16[128,1,6,512]{3,2,1,0:T(8,128)(2,1)S(1)} async-done(((bf16[128,1,6,512]{3,2,1,0:T(8,128)(2,1)}), bf16[128,1,6,512]{3,2,1,0:T(8,128)(2,1)S(1)}, u32[]{:S(2)}, u32[]{:S(2)}) %all-to-all-start.2) | async-done | bytes 786464 | tf_op jit(solution)/shard_map/all_to_all | solution.py:65
  240.8 5.4 %fusion.18 = bf16[128,1,6,512]{3,0,2,1:T(8,128)(2,1)S(1)} fusion(bf16[1,512,1408]{2,1,0:T(8,128)(2,1)S(1)} %copy-done, f32[128,6,1408]{2,0,1:T(8,128)} %fusion.7, bf16[1,1408,512]{2,1,0:T(8,128)(2,1)} %param.16, bf16[128,1,6,512]{3,2,1,0:T(8,128)(2,1)S(1)} %all-to-all-done.2), kind=kOutput, calls=%fused_computation.22 | convolution fusion | flops 2219311104 | bytes 8781824 | tf_op jit(solution)/shard_map/sjmf,jlf->sjml/dot_general | solution.py:71
  246.2 1.5 copy.51
  247.7 6.5 %all-to-all-start.3 = ((bf16[128,1,6,512]{3,2,1,0:T(8,128)(2,1)}), bf16[128,1,6,512]{3,2,1,0:T(8,128)(2,1)S(1)}, u32[]{:S(2)}, u32[]{:S(2)}) async-start(bf16[128,1,6,512]{3,2,1,0:T(8,128)(2,1)} %copy.51), calls=%async_computation.3 | async-start | bytes 2097152 | tf_op jit(solution)/shard_map/all_to_all | solution.py:74
  254.2 4.0 %fusion.15 = bf16[128,1,6,512]{3,0,2,1:T(8,128)(2,1)S(1)} fusion(bf16[1,1408,512]{2,1,0:T(8,128)(2,1)} %param.16, f32[128,6,1408]{2,0,1:T(8,128)} %fusion.7), kind=kOutput, calls=%fused_computation.21 | convolution fusion | flops 1110933504 | bytes 6553600 | tf_op jit(solution)/shard_map/sjmf,jfl->sjml/dot_general | solution.py:47
  258.2 0.0 copy-start.6
  258.3 1.4 copy.46
  259.7 25.4 %all-to-all-done.3 = bf16[128,1,6,512]{3,2,1,0:T(8,128)(2,1)S(1)} async-done(((bf16[128,1,6,512]{3,2,1,0:T(8,128)(2,1)}), bf16[128,1,6,512]{3,2,1,0:T(8,128)(2,1)S(1)}, u32[]{:S(2)}, u32[]{:S(2)}) %all-to-all-start.3) | async-done | bytes 786464 | tf_op jit(solution)/shard_map/all_to_all | solution.py:74
  285.1 6.9 %all-to-all-start.1 = ((bf16[128,1,6,512]{3,2,1,0:T(8,128)(2,1)}), bf16[128,1,6,512]{3,2,1,0:T(8,128)(2,1)}, u32[]{:S(2)}, u32[]{:S(2)}) async-start(bf16[128,1,6,512]{3,2,1,0:T(8,128)(2,1)} %copy.46), calls=%async_computation.1 | async-start | bytes 2097152 | tf_op jit(solution)/shard_map/all_to_all | solution.py:51
  292.0 0.7 copy.42
  292.8 0.1 copy.47
  292.9 0.1 reshape.95
  293.0 0.0 copy-done.6
  293.0 0.1 copy.43
  293.1 0.3 reshape.74
  293.4 2.0 gather_fusion.1
  295.4 0.9 reshape.102
  296.3 26.3 %all-to-all-done.1 = bf16[128,1,6,512]{3,2,1,0:T(8,128)(2,1)} async-done(((bf16[128,1,6,512]{3,2,1,0:T(8,128)(2,1)}), bf16[128,1,6,512]{3,2,1,0:T(8,128)(2,1)}, u32[]{:S(2)}, u32[]{:S(2)}) %all-to-all-start.1) | async-done | bytes 786464 | tf_op jit(solution)/shard_map/all_to_all | solution.py:51
  322.6 1.4 reshape.70
  324.0 2.6 gather_fusion
  326.6 0.0 copy-start.1
  326.6 2.1 reshape.98
  328.7 0.0 copy-start.2
  328.7 1.8 select_reduce_fusion.1
  330.6 1.9 multiply_reduce_fusion
  332.5 0.0 copy-done.1
  332.5 1.6 convolution_convert_fusion
  334.1 0.0 copy-done.2
  334.1 1.6 convolution_convert_fusion.1
  (3 shorter events, 0.0 us)
Async XLA Ops:
  7.2 202.7 %copy-start = (bf16[1,512,1408]{2,1,0:T(8,128)(2,1)S(1)}, bf16[1,512,1408]{2,1,0:T(8,128)(2,1)}, u32[]{:S(2)}) copy-start(bf16[1,512,1408]{2,1,0:T(8,128)(2,1)} %param.15) | copy-start | bytes 4325380
  7.2 92.8 %all-gather.3.cloned.1.call-start = ((), (), s32[]{:S(2)}) async-start(), calls=%async_computation.4 | async-start | bytes 2113536 | tf_op jit(solution)/shard_map/all_gather | solution.py:24
  7.9 187.6 %all-gather.5.cloned.1.call-start = ((), (), s32[]{:S(2)}) async-start(), calls=%async_computation.5 | async-start | bytes 2113536 | tf_op jit(solution)/shard_map/all_gather | solution.py:25
  102.5 10.8 %copy-start.5 = (f32[128,4]{0,1:T(4,128)S(1)}, f32[128,4]{0,1:T(4,128)}, u32[]{:S(2)}) copy-start(f32[128,4]{0,1:T(4,128)} %param.12) | copy-start | bytes 6148
  102.5 93.0 %copy-start.4 = (bf16[128,2048]{1,0:T(8,128)(2,1)S(1)}, bf16[128,2048]{1,0:T(8,128)(2,1)}, u32[]{:S(2)}) copy-start(bf16[128,2048]{1,0:T(8,128)(2,1)} %param.17) | copy-start | bytes 1572868
  103.8 96.6 %all-to-all-start = ((bf16[128,1,6,512]{3,2,1,0:T(8,128)(2,1)}), bf16[128,1,6,512]{3,2,1,0:T(8,128)(2,1)S(1)}, u32[]{:S(2)}, u32[]{:S(2)}) async-start(bf16[128,1,6,512]{3,2,1,0:T(8,128)(2,1)} %bitcast), calls=%async_computation | async-start | bytes 2097152 | tf_op jit(solution)/shard_map/all_to_all | solution.py:42
  195.5 2.1 copy-start.3
  200.3 40.4 %all-to-all-start.2 = ((bf16[128,1,6,512]{3,2,1,0:T(8,128)(2,1)}), bf16[128,1,6,512]{3,2,1,0:T(8,128)(2,1)S(1)}, u32[]{:S(2)}, u32[]{:S(2)}) async-start(bf16[128,1,6,512]{3,2,1,0:T(8,128)(2,1)} %bitcast.9), calls=%async_computation.2 | async-start | bytes 2097152 | tf_op jit(solution)/shard_map/all_to_all | solution.py:65
  247.7 37.4 %all-to-all-start.3 = ((bf16[128,1,6,512]{3,2,1,0:T(8,128)(2,1)}), bf16[128,1,6,512]{3,2,1,0:T(8,128)(2,1)S(1)}, u32[]{:S(2)}, u32[]{:S(2)}) async-start(bf16[128,1,6,512]{3,2,1,0:T(8,128)(2,1)} %copy.51), calls=%async_computation.3 | async-start | bytes 2097152 | tf_op jit(solution)/shard_map/all_to_all | solution.py:74
  258.2 34.7 %copy-start.6 = (pred[128,4]{0,1:T(4,128)(4,1)S(1)}, pred[128,4]{0,1:T(4,128)(4,1)}, u32[]{:S(2)}) copy-start(pred[128,4]{0,1:T(4,128)(4,1)} %get-tuple-element.3) | copy-start | bytes 1540
  285.1 37.5 %all-to-all-start.1 = ((bf16[128,1,6,512]{3,2,1,0:T(8,128)(2,1)}), bf16[128,1,6,512]{3,2,1,0:T(8,128)(2,1)}, u32[]{:S(2)}, u32[]{:S(2)}) async-start(bf16[128,1,6,512]{3,2,1,0:T(8,128)(2,1)} %copy.46), calls=%async_computation.1 | async-start | bytes 2097152 | tf_op jit(solution)/shard_map/all_to_all | solution.py:51
  326.6 5.9 %copy-start.1 = (bf16[2048,512]{1,0:T(8,128)(2,1)S(1)}, bf16[2048,512]{1,0:T(8,128)(2,1)}, u32[]{:S(2)}) copy-start(bf16[2048,512]{1,0:T(8,128)(2,1)} %all-gather.3.cloned.1.call-done) | copy-start | bytes 6291460
  328.7 5.4 %copy-start.2 = (bf16[512,2048]{0,1:T(8,128)(2,1)S(1)}, bf16[512,2048]{0,1:T(8,128)(2,1)}, u32[]{:S(2)}) copy-start(bf16[512,2048]{0,1:T(8,128)(2,1)} %all-gather.5.cloned.1.call-done) | copy-start | bytes 6291460
Sparse Core Ops, SparseCore 0:
  11.1 88.7 all-gather.2
  103.1 92.4 all-gather.4
where the time goes:
time: 343 us
  waiting for transfers between devices  250 us (73%)
  starting transfers between devices  32.5 us (9%)
  matrix products  22.1 us (6%)
  local copies, waits for them, and re-layouts  15.9 us (5%)
  between operations  14.2 us (4%)
  other arithmetic  8.04 us (2%)
    all_gather x1, waiting for transfers between devices, on_device(): lax.all_gather(latent_down, 'ep', axis=0, tiled=True)  87.9 us
    all_gather x1, waiting for transfers between devices, on_device(): lax.all_gather(latent_up, 'ep', axis=1, tiled=True)  81.3 us
    all_to_all x1, waiting for transfers between devices, on_device(): lax.all_to_all(grad_send, 'ep', split_axis=0, concat_axis=0, tiled=True)  27.5 us
    all_to_all x1, waiting for transfers between devices, on_device(): lax.all_to_all(expert_out, 'ep', split_axis=0, concat_axis=0, tiled=True)  26.3 us
    all_to_all x1, waiting for transfers between devices, on_device(): lax.all_to_all(grad_in, 'ep', split_axis=0, concat_axis=0, tiled=True)  25.4 us
    all_to_all x1, starting transfers between devices, on_device(): lax.all_to_all(outbound, 'ep', split_axis=0, concat_axis=0, tiled=True)  9.51 us
    all_to_all x1, starting transfers between devices, on_device(): lax.all_to_all(grad_send, 'ep', split_axis=0, concat_axis=0, tiled=True)  9.5 us
    all_to_all x1, starting transfers between devices, on_device(): lax.all_to_all(expert_out, 'ep', split_axis=0, concat_axis=0, tiled=True)  6.94 us
  transfers between devices with their start and end apart: 6, of which 5 were waited for; matrix products, arithmetic and copies ran while one was open for 8% of the time, Pallas kernels for 0%

commit v1 on v0

--- a/solution.py
+++ b/solution.py
@@ -21,7 +21,9 @@
     experts = local_experts * ep_size
     capacity = max(2, (3 * tok_rows * top_count + 2 * experts - 1) // (2 * experts))
     full_down, full_up = (
-        lax.all_gather(latent_down, "ep", axis=0, tiled=True),
+        jnp.concatenate(
+            lax.all_to_all(jnp.stack([latent_down] * lax.axis_size("ep")), "ep", 0, 0), axis=0
+        ),
         lax.all_gather(latent_up, "ep", axis=1, tiled=True),
     )
     latent = jnp.dot(tokens, full_down, preferred_element_type=jnp.float32).astype(jnp.bfloat16)

time: 343 us -> 286 us (0.83)
  waiting for transfers between devices: 250 us -> 169 us
  starting transfers between devices: 32.5 us -> 51.2 us
  matrix products: 22.1 us -> 26 us
    all_gather x1 -> x0, waiting for transfers between devices: 87.9 us -> none  [on_device(): lax.all_gather(latent_down, 'ep', axis=0, tiled=True)]
    all_to_all x0 -> x1, waiting for transfers between devices: none -> 46.3 us  [on_device(): lax.all_to_all(jnp.stack([latent_down] * lax.axis_size('ep')), 'ep', 0, 0)]
    all_gather x1, waiting for transfers between devices: 81.3 us -> 47.7 us  [on_device(): lax.all_gather(latent_up, 'ep', axis=1, tiled=True)]
    all_to_all x0 -> x1, starting transfers between devices: none -> 18.6 us  [on_device(): lax.all_to_all(jnp.stack([latent_down] * lax.axis_size('ep')), 'ep', 0, 0)]
    all_to_all x1, waiting for transfers between devices: 26.3 us -> 21.4 us  [on_device(): lax.all_to_all(expert_out, 'ep', split_axis=0, concat_axis=0, tiled=True)]
  transfers between devices with their start and end apart: 6 -> 6, of which waited for: 5 -> 5; matrix products, arithmetic and copies ran while one was open for 8% -> 12% of each run, Pallas kernels for 0% -> 0%
where the time goes in v1:
time: 286 us; the launch traced here: 285 us
  waiting for transfers between devices  169 us (59%)
  starting transfers between devices  51.2 us (18%)
  matrix products  26 us (9%)
  local copies, waits for them, and re-layouts  17.9 us (6%)
  between operations  14.2 us (5%)
  other arithmetic  6.81 us (2%)
    all_gather x1, waiting for transfers between devices, on_device(): lax.all_gather(latent_up, 'ep', axis=1, tiled=True)  47.7 us
    all_to_all x1, waiting for transfers between devices, on_device(): lax.all_to_all(jnp.stack([latent_down] * lax.axis_size('ep')), 'ep', 0, 0)  46.3 us
    all_to_all x1, waiting for transfers between devices, on_device(): lax.all_to_all(grad_send, 'ep', split_axis=0, concat_axis=0, tiled=True)  27.5 us
    all_to_all x1, waiting for transfers between devices, on_device(): lax.all_to_all(grad_in, 'ep', split_axis=0, concat_axis=0, tiled=True)  25.4 us
    all_to_all x1, waiting for transfers between devices, on_device(): lax.all_to_all(expert_out, 'ep', split_axis=0, concat_axis=0, tiled=True)  21.4 us
    all_to_all x1, starting transfers between devices, on_device(): lax.all_to_all(jnp.stack([latent_down] * lax.axis_size('ep')), 'ep', 0, 0)  18.6 us
    all_to_all x1, starting transfers between devices, on_device(): lax.all_to_all(grad_send, 'ep', split_axis=0, concat_axis=0, tiled=True)  10.6 us
    all_to_all x1, starting transfers between devices, on_device(): lax.all_to_all(outbound, 'ep', split_axis=0, concat_axis=0, tiled=True)  9.07 us
  transfers between devices with their start and end apart: 6, of which 5 were waited for; matrix products, arithmetic and copies ran while one was open for 12% of the time, Pallas kernels for 0%

profile of v1, /device:TPU:1, one launch (start us, length us, event | category | flops | bytes accessed | tf_op | source)
XLA Modules:
  0.0 285.2 jit_solution(16598632800757022513)
XLA Ops:
  7.2 0.0 copy-start
  7.2 2.4 stack.2
  9.6 0.0 copy-start.5
  9.6 18.6 %all-to-all-start = ((bf16[128,16,512]{2,1,0:T(8,128)(2,1)}), bf16[128,16,512]{2,1,0:T(8,128)(2,1)S(1)}, u32[]{:S(2)}, u32[]{:S(2)}) async-start(bf16[128,16,512]{2,1,0:T(8,128)(2,1)} %stack.2), calls=%async_computation | async-start | bytes 4194304 | tf_op jit(solution)/shard_map/all_to_all | solution.py:25
  28.2 0.0 all-gather.2.cloned.1.call-start
  28.2 0.7 all-gather.2.cloned.1.call-update
  28.9 0.0 copy-done.5
  28.9 0.8 convert_reduce_fusion
  29.7 1.6 reduce_window_sum.11
  31.3 0.9 sub.7
  32.2 0.2 select_reduce_fusion.2
  32.4 0.9 fusion.2
  33.3 46.3 %all-to-all-done = bf16[128,16,512]{2,1,0:T(8,128)(2,1)S(1)} async-done(((bf16[128,16,512]{2,1,0:T(8,128)(2,1)}), bf16[128,16,512]{2,1,0:T(8,128)(2,1)S(1)}, u32[]{:S(2)}, u32[]{:S(2)}) %all-to-all-start) | async-done | bytes 2097184 | tf_op jit(solution)/shard_map/all_to_all | solution.py:25
  79.6 0.0 copy-start.1
  79.7 3.3 %convolution_convert_fusion.3 = bf16[768,512]{1,0:T(8,128)(2,1)} fusion(pred[768,128]{1,0:T(8,128)(4,1)} %fusion.2, bf16[128,2048]{1,0:T(8,128)(2,1)} %param.10, bf16[2048,512]{1,0:T(8,128)(2,1)S(1)} %bitcast.55), kind=kOutput, calls=%fused_computation.20 | convolution fusion | flops 369557504 | bytes 3506176 | tf_op jit(solution)/shard_map/dot_general | solution.py:40
  82.9 0.0 copy-start.6
  82.9 2.2 reshape.72
  85.1 0.0 copy-done.1
  85.1 0.0 copy-start.4
  85.1 9.1 %all-to-all-start.1 = ((bf16[128,1,6,512]{3,2,1,0:T(8,128)(2,1)}), bf16[128,1,6,512]{3,2,1,0:T(8,128)(2,1)S(1)}, u32[]{:S(2)}, u32[]{:S(2)}) async-start(bf16[128,1,6,512]{3,2,1,0:T(8,128)(2,1)} %bitcast.57), calls=%async_computation.1 | async-start | bytes 2097152 | tf_op jit(solution)/shard_map/all_to_all | solution.py:44
  94.2 0.0 copy-done.6
  94.2 0.9 select_reduce_fusion
  95.1 47.7 %all-gather.2.cloned.1.call-done = bf16[512,2048]{0,1:T(8,128)(2,1)} async-done(((bf16[512,16]{0,1:T(8,128)(2,1)}), bf16[512,2048]{0,1:T(8,128)(2,1)}) %all-gather.2.cloned.1.call-update) | async-done | bytes 2097168 | tf_op jit(solution)/shard_map/all_gather | solution.py:27
  142.8 0.0 copy-done.4
  142.8 0.0 copy-start.3
  142.8 2.1 fusion.33
  144.9 0.0 copy-done.3
  144.9 1.4 convolution_convert_fusion.2
  146.3 1.3 reshape.77
  147.6 0.0 all-to-all-done.1
  147.6 10.6 %all-to-all-start.3 = ((bf16[128,1,6,512]{3,2,1,0:T(8,128)(2,1)}), bf16[128,1,6,512]{3,2,1,0:T(8,128)(2,1)S(1)}, u32[]{:S(2)}, u32[]{:S(2)}) async-start(bf16[128,1,6,512]{3,2,1,0:T(8,128)(2,1)} %bitcast.10), calls=%async_computation.3 | async-start | bytes 2097152 | tf_op jit(solution)/shard_map/all_to_all | solution.py:67
  158.3 0.0 copy-done
  158.3 3.4 %fusion.7 = f32[128,6,1408]{2,0,1:T(8,128)} fusion(bf16[1,512,1408]{2,1,0:T(8,128)(2,1)S(1)} %copy-done, bf16[128,1,6,512]{3,2,1,0:T(8,128)(2,1)S(1)} %all-to-all-done.1), kind=kOutput, calls=%fused_computation.15 | convolution fusion | flops 1107296256 | bytes 6553600 | tf_op jit(solution)/shard_map/sjml,jlf->sjmf/dot_general | solution.py:42
  161.7 27.5 %all-to-all-done.3 = bf16[128,1,6,512]{3,2,1,0:T(8,128)(2,1)S(1)} async-done(((bf16[128,1,6,512]{3,2,1,0:T(8,128)(2,1)}), bf16[128,1,6,512]{3,2,1,0:T(8,128)(2,1)S(1)}, u32[]{:S(2)}, u32[]{:S(2)}) %all-to-all-start.3) | async-done | bytes 786464 | tf_op jit(solution)/shard_map/all_to_all | solution.py:67
  189.2 5.4 %fusion.18 = bf16[128,1,6,512]{3,0,2,1:T(8,128)(2,1)S(1)} fusion(bf16[1,512,1408]{2,1,0:T(8,128)(2,1)S(1)} %copy-done, f32[128,6,1408]{2,0,1:T(8,128)} %fusion.7, bf16[1,1408,512]{2,1,0:T(8,128)(2,1)} %param.16, bf16[128,1,6,512]{3,2,1,0:T(8,128)(2,1)S(1)} %all-to-all-done.3), kind=kOutput, calls=%fused_computation.22 | convolution fusion | flops 2219311104 | bytes 8781824 | tf_op jit(solution)/shard_map/sjmf,jlf->sjml/dot_general | solution.py:73
  194.6 1.5 copy.51
  196.1 6.5 %all-to-all-start.4 = ((bf16[128,1,6,512]{3,2,1,0:T(8,128)(2,1)}), bf16[128,1,6,512]{3,2,1,0:T(8,128)(2,1)S(1)}, u32[]{:S(2)}, u32[]{:S(2)}) async-start(bf16[128,1,6,512]{3,2,1,0:T(8,128)(2,1)} %copy.51), calls=%async_computation.4 | async-start | bytes 2097152 | tf_op jit(solution)/shard_map/all_to_all | solution.py:76
  202.6 4.1 %fusion.15 = bf16[128,1,6,512]{3,0,2,1:T(8,128)(2,1)S(1)} fusion(bf16[1,1408,512]{2,1,0:T(8,128)(2,1)} %param.16, f32[128,6,1408]{2,0,1:T(8,128)} %fusion.7), kind=kOutput, calls=%fused_computation.21 | convolution fusion | flops 1110933504 | bytes 6553600 | tf_op jit(solution)/shard_map/sjmf,jfl->sjml/dot_general | solution.py:49
  206.7 1.4 copy.46
  208.1 25.4 %all-to-all-done.4 = bf16[128,1,6,512]{3,2,1,0:T(8,128)(2,1)S(1)} async-done(((bf16[128,1,6,512]{3,2,1,0:T(8,128)(2,1)}), bf16[128,1,6,512]{3,2,1,0:T(8,128)(2,1)S(1)}, u32[]{:S(2)}, u32[]{:S(2)}) %all-to-all-start.4) | async-done | bytes 786464 | tf_op jit(solution)/shard_map/all_to_all | solution.py:76
  233.5 0.0 copy-start.2
  233.5 1.0 copy-done.2
  234.5 6.5 %all-to-all-start.2 = ((bf16[128,1,6,512]{3,2,1,0:T(8,128)(2,1)}), bf16[128,1,6,512]{3,2,1,0:T(8,128)(2,1)S(1)}, u32[]{:S(2)}, u32[]{:S(2)}) async-start(bf16[128,1,6,512]{3,2,1,0:T(8,128)(2,1)} %copy.46), calls=%async_computation.2 | async-start | bytes 2097152 | tf_op jit(solution)/shard_map/all_to_all | solution.py:53
  241.0 0.1 copy.42
  241.1 0.1 copy.47
  241.3 0.1 reshape.101
  241.4 0.1 copy.43
  241.5 1.4 reshape.80
  242.9 2.6 gather_fusion.1
  245.5 1.2 reshape.108
  246.7 0.6 select_reduce_fusion.1
  247.4 3.2 %convolution_convert_fusion = bf16[128,2048]{1,0:T(8,128)(2,1)} fusion(bf16[128,512]{1,0:T(8,128)(2,1)S(1)} %select_reduce_fusion.1, bf16[2048,512]{1,0:T(8,128)(2,1)} %bitcast.56), kind=kOutput, calls=%fused_computation.4 | convolution fusion | flops 268697600 | bytes 2752512 | tf_op jit(solution)/shard_map/dot_general | solution.py:8
  250.6 21.4 %all-to-all-done.2 = bf16[128,1,6,512]{3,2,1,0:T(8,128)(2,1)S(1)} async-done(((bf16[128,1,6,512]{3,2,1,0:T(8,128)(2,1)}), bf16[128,1,6,512]{3,2,1,0:T(8,128)(2,1)S(1)}, u32[]{:S(2)}, u32[]{:S(2)}) %all-to-all-start.2) | async-done | bytes 786464 | tf_op jit(solution)/shard_map/all_to_all | solution.py:53
  271.9 0.3 reshape.76
  272.2 2.0 gather_fusion
  274.2 0.1 reshape.104
  274.3 0.9 multiply_reduce_fusion
  275.2 3.2 %convolution_convert_fusion.1 = bf16[128,2048]{1,0:T(8,128)(2,1)} fusion(bf16[512,2048]{0,1:T(8,128)(2,1)} %all-gather.2.cloned.1.call-done, bf16[128,512]{1,0:T(8,128)(2,1)S(1)} %multiply_reduce_fusion), kind=kOutput, calls=%fused_computation.5 | convolution fusion | flops 268697600 | bytes 2752512 | tf_op jit(solution)/shard_map/dot_general | solution.py:60
  (3 shorter events, 0.0 us)
Async XLA Ops:
  7.2 151.1 %copy-start = (bf16[1,512,1408]{2,1,0:T(8,128)(2,1)S(1)}, bf16[1,512,1408]{2,1,0:T(8,128)(2,1)}, u32[]{:S(2)}) copy-start(bf16[1,512,1408]{2,1,0:T(8,128)(2,1)} %param.15) | copy-start | bytes 4325380
  9.6 19.3 %copy-start.5 = (s32[128,4]{0,1:T(4,128)S(1)}, s32[128,4]{0,1:T(4,128)}, u32[]{:S(2)}) copy-start(s32[128,4]{0,1:T(4,128)} %param.11) | copy-start | bytes 6148
  9.6 70.0 %all-to-all-start = ((bf16[128,16,512]{2,1,0:T(8,128)(2,1)}), bf16[128,16,512]{2,1,0:T(8,128)(2,1)S(1)}, u32[]{:S(2)}, u32[]{:S(2)}) async-start(bf16[128,16,512]{2,1,0:T(8,128)(2,1)} %stack.2), calls=%async_computation | async-start | bytes 4194304 | tf_op jit(solution)/shard_map/all_to_all | solution.py:25
  28.2 114.7 %all-gather.2.cloned.1.call-start = ((), (), s32[]{:S(2)}) async-start(), calls=%async_computation.5 | async-start | bytes 2113536 | tf_op jit(solution)/shard_map/all_gather | solution.py:27
  79.6 5.5 %copy-start.1 = (bf16[128,16,512]{2,1,0:T(8,128)(2,1)}, bf16[128,16,512]{2,1,0:T(8,128)(2,1)S(1)}, u32[]{:S(2)}) copy-start(bf16[128,16,512]{2,1,0:T(8,128)(2,1)S(1)} %all-to-all-done) | copy-start | bytes 6291460
  82.9 11.3 %copy-start.6 = (f32[128,4]{0,1:T(4,128)S(1)}, f32[128,4]{0,1:T(4,128)}, u32[]{:S(2)}) copy-start(f32[128,4]{0,1:T(4,128)} %param.12) | copy-start | bytes 6148
  85.1 57.7 %copy-start.4 = (bf16[128,2048]{1,0:T(8,128)(2,1)S(1)}, bf16[128,2048]{1,0:T(8,128)(2,1)}, u32[]{:S(2)}) copy-start(bf16[128,2048]{1,0:T(8,128)(2,1)} %param.17) | copy-start | bytes 1572868
  85.1 62.5 %all-to-all-start.1 = ((bf16[128,1,6,512]{3,2,1,0:T(8,128)(2,1)}), bf16[128,1,6,512]{3,2,1,0:T(8,128)(2,1)S(1)}, u32[]{:S(2)}, u32[]{:S(2)}) async-start(bf16[128,1,6,512]{3,2,1,0:T(8,128)(2,1)} %bitcast.57), calls=%async_computation.1 | async-start | bytes 2097152 | tf_op jit(solution)/shard_map/all_to_all | solution.py:44
  142.8 2.1 copy-start.3
  147.6 41.5 %all-to-all-start.3 = ((bf16[128,1,6,512]{3,2,1,0:T(8,128)(2,1)}), bf16[128,1,6,512]{3,2,1,0:T(8,128)(2,1)S(1)}, u32[]{:S(2)}, u32[]{:S(2)}) async-start(bf16[128,1,6,512]{3,2,1,0:T(8,128)(2,1)} %bitcast.10), calls=%async_computation.3 | async-start | bytes 2097152 | tf_op jit(solution)/shard_map/all_to_all | solution.py:67
  196.1 37.4 %all-to-all-start.4 = ((bf16[128,1,6,512]{3,2,1,0:T(8,128)(2,1)}), bf16[128,1,6,512]{3,2,1,0:T(8,128)(2,1)S(1)}, u32[]{:S(2)}, u32[]{:S(2)}) async-start(bf16[128,1,6,512]{3,2,1,0:T(8,128)(2,1)} %copy.51), calls=%async_computation.4 | async-start | bytes 2097152 | tf_op jit(solution)/shard_map/all_to_all | solution.py:76
  233.5 1.0 copy-start.2
  234.5 37.4 %all-to-all-start.2 = ((bf16[128,1,6,512]{3,2,1,0:T(8,128)(2,1)}), bf16[128,1,6,512]{3,2,1,0:T(8,128)(2,1)S(1)}, u32[]{:S(2)}, u32[]{:S(2)}) async-start(bf16[128,1,6,512]{3,2,1,0:T(8,128)(2,1)} %copy.46), calls=%async_computation.2 | async-start | bytes 2097152 | tf_op jit(solution)/shard_map/all_to_all | solution.py:53
Sparse Core Ops, SparseCore 0:
  32.1 110.6 all-gather.1
